TPU v7x, 32 devices: a whole 2x2x4 slice. The times are simulated.
32 devices in a mesh: lsec: 8 (over z, x), rsec: 4 (over y, core).
Axes of the slice: x: 2, y: 2, z: 4, core: 2. Of those that a mesh axis runs over, the one named last changes fastest.
Arguments:
- wavefunction: bfloat16 [2, 8192, 8192], P(None, 'lsec', 'rsec'), may hold values from -6 to 6
- left_tiles: bfloat16 [4, 64, 2, 128, 128], P(None, 'lsec'), may hold values from -0.5 to 0.5
- left_source_sector: int32 [4, 64, 2], replicated, may hold values from 0 to 63
- left_weight: float32 [4, 64, 2], replicated, may hold values from -1 to 1
- left_sizes: int32 [64], replicated, may hold values from 1 to 128, 4096 in all
- right_tiles: bfloat16 [4, 64, 4, 128, 128], P(None, 'rsec'), may hold values from -0.5 to 0.5
- right_source: int32 [4, 64, 4], P(None, 'rsec'), may hold values from 0 to 63
- right_weight: float32 [4, 64, 4], P(None, 'rsec'), may hold values from -1 to 1
- right_sizes: int32 [64], replicated, may hold values from 1 to 128, 4096 in all
Outputs:
- sigma: bfloat16 [2, 8192, 8192], P(None, 'lsec', 'rsec')
Inputs may be any that keep to these rules, and one draw needn't show every extreme that they name: `left_sizes`: left sector sizes sum to 4096; the largest is exactly 128. `right_sizes`: right sector sizes sum to 4096; the largest is exactly 128.
All inputs are finite; a program needn't handle non-finite values.
Results may differ from a plain program's by a relative error of at most 0.0064.
Values may be sent and summed in bfloat16 or wider, within the bound.
No kernel may reach another device: no remote copies, remote signals or barrier semaphores. Data moves between devices by JAX's collectives and lax.ppermute only.
A program may use at most 320 MiB of HBM per device.

v0:
```python
import jax
import jax.numpy as jnp
from jax import lax
from jax.sharding import PartitionSpec as P


def sector_mask(sizes, tile):
    offsets = jnp.arange(tile, dtype=jnp.int32)
    return (offsets[None, :] < sizes[:, None]).reshape(-1)


def scaled_tiles(tiles, weight):
    return (tiles.astype(jnp.float32) * weight[..., None, None]).astype(jnp.bfloat16)


def weighted_right(selected_rows, scaled):
    return jnp.einsum("vlqbs,qbts->vlqt", selected_rows, scaled, preferred_element_type=jnp.float32)


def left_rows(arranged, product_fragments, source, weight):
    total = None
    for term in range(product_fragments.shape[0]):
        selected_rows = jnp.take(arranged[:, :, :, term, :], source[term], axis=1)
        scaled = scaled_tiles(product_fragments[term], weight[term])
        part = jnp.einsum(
            "mbij,vmbjc->vmic", scaled, selected_rows, preferred_element_type=jnp.float32
        )
        total = part if total is None else total + part
    return total.reshape(total.shape[0], -1, total.shape[-1])


def local(
    wavefunction,
    left_tiles,
    left_source_sector,
    left_weight,
    left_sizes,
    right_tiles,
    right_source,
    right_weight,
    right_sizes,
):
    vectors, rows_local, cols_local = wavefunction.shape
    terms_count = right_tiles.shape[0]
    tile = right_tiles.shape[3]
    left_count = left_sizes.shape[0]
    right_count = right_sizes.shape[0]
    left_local = rows_local // tile
    right_local = cols_local // tile
    left_devices = lax.axis_size("lsec")
    width = cols_local // left_devices
    left_place = lax.axis_index("lsec")
    right_place = lax.axis_index("rsec")
    row_keep_mask = sector_mask(
        lax.dynamic_slice_in_dim(left_sizes, left_place * left_local, left_local), tile
    )
    col_keep = sector_mask(
        lax.dynamic_slice_in_dim(right_sizes, right_place * right_local, right_local), tile
    )
    masked = jnp.where(
        row_keep_mask[None, :, None] & col_keep[None, None, :],
        wavefunction,
        jnp.zeros((), wavefunction.dtype),
    )
    right_scaled = scaled_tiles(right_tiles, right_weight)
    gathered = lax.all_gather(masked, "rsec", axis=2, tiled=True)
    sector_block_list = gathered.reshape(vectors, rows_local, right_count, tile)
    products = []
    for term in range(terms_count):
        selected_rows = jnp.take(sector_block_list, right_source[term], axis=2)
        products.append(weighted_right(selected_rows, right_scaled[term]))
    rounded = [
        item.astype(jnp.bfloat16).reshape(vectors, rows_local, left_devices, width)
        for item in products
    ]
    outgoing = jnp.stack(rounded, axis=3)
    exchanged_values = lax.all_to_all(
        outgoing.reshape(vectors, rows_local, -1), "lsec", split_axis=2, concat_axis=1, tiled=True
    )
    arranged = exchanged_values.reshape(vectors, left_count, tile, terms_count, width)
    sigma_part = left_rows(
        arranged,
        lax.all_gather(left_tiles, "lsec", axis=1, tiled=True),
        left_source_sector,
        left_weight,
    )
    row_all = sector_mask(left_sizes, tile)
    columns = right_place * cols_local + left_place * width + jnp.arange(width, dtype=jnp.int32)
    column_sizes = jnp.take(right_sizes, columns // tile)
    column_keep = columns % tile < column_sizes
    result = jnp.where(
        row_all[None, :, None] & column_keep[None, None, :],
        sigma_part,
        jnp.zeros((), sigma_part.dtype),
    )
    return lax.all_to_all(
        result.astype(jnp.bfloat16), "lsec", split_axis=1, concat_axis=2, tiled=True
    )


def solution(mesh):
    return jax.shard_map(
        local,
        mesh=mesh,
        in_specs=(
            P(None, "lsec", "rsec"),
            P(None, "lsec", None, None, None),
            P(),
            P(),
            P(),
            P(None, "rsec", None, None, None),
            P(None, "rsec", None),
            P(None, "rsec", None),
            P(),
        ),
        out_specs=P(None, "lsec", "rsec"),
        check_vma=False,
    )
```

profile of v0, /device:TPU:0, one launch (start us, length us, event | category | flops | bytes accessed | tf_op | source)
XLA Modules:
  0.0 2056.9 jit_solution(6572497530805812091)
XLA Ops:
  7.4 0.7 dynamic_slice.6
  8.2 0.7 dynamic_slice.7
  9.0 11.8 copy.119
  20.8 1.1 broadcast_and_fusion
  21.9 8.1 broadcast_select_fusion
  30.2 0.1 copy.117
  30.3 0.1 copy.118
  31.1 0.7 copy.134
  31.9 9.6 multiply_convert_fusion
  41.4 192.9 %all-gather.3.cloned.1.call-done = bf16[2,1024,8192]{1,2,0:T(8,128)(2,1)} async-done(((bf16[2,1024,2048]{1,2,0:T(8,128)(2,1)}), bf16[2,1024,8192]{1,2,0:T(8,128)(2,1)}) %all-gather.3.cloned.1.call-update) | async-done | bytes 33554448 | tf_op jit(solution)/shard_map/all_gather | solution.py:66
  234.4 41.9 %copy.121 = bf16[2,1024,64,128]{3,1,2,0:T(8,128)(2,1)} copy(bf16[2,1024,64,128]{1,3,2,0:T(8,128)(2,1)} %bitcast.272) | data formatting | bytes 67108864 | tf_op jit(solution)/shard_map/reshape | solution.py:67
  276.3 22.8 %gather_fusion.1 = bf16[64,2,1024,128]{3,2,1,0:T(8,128)(2,1)} fusion(bf16[2,1024,64,128]{3,1,2,0:T(8,128)(2,1)} %copy.121, s32[1024]{0:T(1024)S(1)} %pad_clamp_fusion.7), kind=kCustom, calls=%fused_computation.clone | custom fusion | bytes 67109120 | tf_op jit(solution)/shard_map/jit(_take)/gather | solution.py:70
  299.1 18.8 fusion.38
  317.9 8.3 copy.123
  326.2 22.7 %gather_fusion.2 = bf16[64,2,1024,128]{3,2,1,0:T(8,128)(2,1)} fusion(bf16[2,1024,64,128]{3,1,2,0:T(8,128)(2,1)} %copy.121, s32[1024]{0:T(1024)S(1)} %pad_clamp_fusion.6), kind=kCustom, calls=%fused_computation.2.clone | custom fusion | bytes 67109120 | tf_op jit(solution)/shard_map/jit(_take)/gather | solution.py:70
  348.9 18.8 fusion.39
  367.7 8.2 copy.128
  375.9 23.0 %gather_fusion.3 = bf16[64,2,1024,128]{3,2,1,0:T(8,128)(2,1)} fusion(bf16[2,1024,64,128]{3,1,2,0:T(8,128)(2,1)} %copy.121, s32[1024]{0:T(1024)S(1)} %pad_clamp_fusion.5), kind=kCustom, calls=%fused_computation.3.clone | custom fusion | bytes 67109120 | tf_op jit(solution)/shard_map/jit(_take)/gather | solution.py:70
  398.9 18.8 fusion.40
  417.7 8.3 copy.133
  426.0 22.8 %gather_fusion.4 = bf16[64,2,1024,128]{3,2,1,0:T(8,128)(2,1)} fusion(bf16[2,1024,64,128]{3,1,2,0:T(8,128)(2,1)} %copy.121, s32[1024]{0:T(1024)S(1)} %pad_clamp_fusion.4), kind=kCustom, calls=%fused_computation.4.clone | custom fusion | bytes 67109120 | tf_op jit(solution)/shard_map/jit(_take)/gather | solution.py:70
  448.8 18.8 fusion.41
  467.7 8.2 copy.138
  475.9 22.7 %pad_maximum_fusion = bf16[2,1024,8,4,256]{1,4,2,0,3:T(8,128)(2,1)} fusion(bf16[2,1024,8,1,256]{1,4,2,0,3:T(8,128)(2,1)} %bitcast.282, bf16[2,1024,8,1,256]{1,4,2,0,3:T(8,128)(2,1)} %bitcast.281, bf16[2,1024,8,1,256]{1,4,2,0,3:T(8,128)(2,1)} %bitcast.280, bf16[2,1024,8,1,256]{1,4,2,0,3:T(8,128)(2,1)} %bitcast.279), kind=kLoop, calls=%fused_computation.9 | loop fusion | flops 50331648 | bytes 67108864 | tf_op jit(solution)/shard_map/stack | solution.py:76
  498.5 22.6 %copy.139 = bf16[2,1024,8,4,256]{1,4,3,2,0:T(8,128)(2,1)} copy(bf16[2,1024,8,4,256]{1,4,2,0,3:T(8,128)(2,1)} %pad_maximum_fusion) | data formatting | bytes 67108864 | tf_op jit(solution)/shard_map/stack | solution.py:76
  521.2 60.1 %copy.140 = bf16[2,1024,8192]{1,0,2:T(2,128)(2,1)} copy(bf16[2,1024,8192]{1,2,0:T(8,128)(2,1)} %bitcast.262) | data formatting | bytes 67108864 | tf_op jit(solution)/shard_map/reshape | solution.py:78
  581.3 7.2 all-to-all-start
  588.6 0.5 all-gather.5.cloned.1.call-update
  589.2 0.1 reshape.375
  589.5 0.1 copy.157
  589.7 0.1 reshape.371
  589.9 0.1 copy.152
  590.2 0.1 reshape.367
  590.3 0.7 copy.150
  591.0 0.7 copy.147
  591.8 0.1 reshape.363
  591.9 0.7 copy.145
  592.6 0.7 copy.116
  593.4 2.3 gather_fusion
  595.8 5.0 broadcast_and_fusion.1
  600.9 913.2 %all-to-all-done = bf16[2,1024,8192]{1,0,2:T(2,128)(2,1)} async-done(((bf16[2,1024,8192]{1,0,2:T(2,128)(2,1)}), bf16[2,1024,8192]{1,0,2:T(2,128)(2,1)}, u32[]{:S(2)}, u32[]{:S(2)}) %all-to-all-start) | async-done | bytes 33554464 | tf_op jit(solution)/shard_map/all_to_all | solution.py:77
  1514.0 23.2 %copy.141 = bf16[2,1024,8192]{1,2,0:T(8,128)(2,1)} copy(bf16[2,1024,8192]{1,0,2:T(2,128)(2,1)} %all-to-all-done) | data formatting | bytes 67108864 | tf_op jit(solution)/shard_map/all_to_all | solution.py:77
  1537.2 30.9 %copy.142 = bf16[2,8,1024,1024]{2,1,3,0:T(8,128)(2,1)} copy(bf16[2,8,1024,1024]{2,3,1,0:T(8,128)(2,1)} %bitcast.263) | data formatting | bytes 67108864 | tf_op jit(solution)/shard_map/all_to_all | solution.py:77
  1568.1 49.3 %reshape.253 = bf16[2,64,128,4,256]{2,1,4,3,0:T(8,128)(2,1)} reshape(bf16[2,8,1024,1024]{2,1,3,0:T(8,128)(2,1)} %copy.142) | data formatting | bytes 67108864 | tf_op jit(solution)/shard_map/reshape | solution.py:80
  1617.4 22.1 %fusion.84 = (bf16[2,64,128,1,256]{2,1,4,3,0:T(8,128)(2,1)}, bf16[2,64,128,1,256]{2,1,4,3,0:T(8,128)(2,1)}, bf16[2,64,128,1,256]{2,1,4,3,0:T(8,128)(2,1)}, bf16[2,64,128,1,256]{2,1,4,3,0:T(8,128)(2,1)}) fusion(bf16[2,64,128,4,256]{2,1,4,3,0:T(8,128)(2,1)} %reshape.253), kind=kLoop, calls=%fused_computation.148 | loop fusion | bytes 67108864 | tf_op jit(solution)/shard_map/slice | solution.py:23
  1639.5 12.5 copy.158
  1652.0 12.4 copy.153
  1664.5 12.4 copy.148
  1676.9 12.5 copy.143
  1689.4 11.8 gather_fusion.8
  1701.2 11.8 gather_fusion.7
  1713.0 11.8 gather_fusion.6
  1724.8 11.7 gather_fusion.5
  1736.5 12.4 fusion.18
  1748.9 12.2 fusion.20
  1761.1 12.3 fusion.22
  1773.4 26.8 %fusion.16 = bf16[2,64,128,256]{3,2,0,1:T(8,128)(2,1)} fusion(f32[64,2,256,128,1]{2,3,1,4,0:T(8,128)} %fusion.18, f32[64,2,256,128,1]{2,3,1,4,0:T(8,128)} %fusion.20, f32[64,2,256,128,1]{2,3,1,4,0:T(8,128)} %fusion.22, bf16[64,2,2,128,256]{4,3,2,1,0:T(8,128)(2,1)} %bitcast.267, pred[64,2]{1,0:T(8,128)(4,1)S(1)} %copy-done.5, ...), kind=kOutput, calls=%fused_computation.27 | convolution fusion | flops 2178940928 | bytes 79692416 | tf_op jit(solution)/shard_map/mbij,vmbjc->vmic/dot_general | solution.py:25
  1800.3 7.9 copy.162
  1808.2 8.7 fusion.17
  1816.9 14.5 copy.163
  1831.4 186.7 %all_to_all.33 = bf16[2,8192,256]{2,0,1:T(2,128)(2,1)} all-to-all(bf16[2,8192,256]{2,0,1:T(2,128)(2,1)S(1)} %copy.163), channel_id=1, replica_groups=mesh['lsec'=8,'rsec'=4] {'lsec'}, dimensions={1} | all-to-all | bytes 16777216 | tf_op jit(solution)/shard_map/all_to_all | solution.py:96
  2018.1 7.9 copy.164
  2026.0 11.7 copy.165
  2037.7 11.6 copy.166
  (63 shorter events, 1.9 us)
Async XLA Ops:
  7.4 227.0 %all-gather.3.cloned.1.call-start = ((), (), s32[]{:S(2)}) async-start(), calls=%async_computation.2 | async-start | bytes 41943040 | tf_op jit(solution)/shard_map/all_gather | solution.py:66
  20.8 9.2 copy-start.6
  20.8 9.4 copy-start.8
  426.0 22.8 %copy-start.10 = (pred[16,4]{1,0:T(8,128)(4,1)S(1)}, pred[16,4]{1,0:T(8,128)(4,1)}, u32[]{:S(2)}) copy-start(pred[16,4]{1,0:T(8,128)(4,1)} %copy.134) | copy-start | bytes 196
  581.3 7.8 copy-start.7
  581.3 8.1 copy-start.9
  581.3 12.1 copy-start
  581.3 14.4 copy-start.11
  581.3 932.7 %all-to-all-start = ((bf16[2,1024,8192]{1,0,2:T(2,128)(2,1)}), bf16[2,1024,8192]{1,0,2:T(2,128)(2,1)}, u32[]{:S(2)}, u32[]{:S(2)}) async-start(bf16[2,1024,8192]{1,0,2:T(2,128)(2,1)} %copy.140), calls=%async_computation | async-start | bytes 67108864 | tf_op jit(solution)/shard_map/all_to_all | solution.py:77
  588.5 1148.0 %all-gather.5.cloned.1.call-start = ((), (), s32[]{:S(2)}) async-start(), calls=%async_computation.3 | async-start | bytes 18874368 | tf_op jit(solution)/shard_map/all_gather | solution.py:83
  1748.9 12.2 copy-start.2
  1748.9 12.2 copy-start.4
  1761.1 12.3 copy-start.3
  1761.1 12.3 copy-start.5
  1800.3 7.9 copy-start.1
Sparse Core Ops, SparseCore 0:
  30.1 204.2 all-gather.2
Sparse Core Ops, SparseCore 1:
  591.2 813.8 all-gather.4
where the time goes:
time: 2070 us; the launch traced here: 2060 us
  waiting for transfers between devices  1110 us (54%)
  local copies, waits for them, and re-layouts  546 us (26%)
  blocking collectives  187 us (9%)
  matrix products  139 us (7%)
  other arithmetic  55.5 us (3%)
    all_to_all x1, waiting for transfers between devices, local(): lax.all_to_all(outgoing.reshape(vectors, rows_local, -1), 'lsec', split_a...  913 us
    all_gather x1, waiting for transfers between devices, local(): gathered = lax.all_gather(masked, 'rsec', axis=2, tiled=True)  193 us
    all_to_all x1, blocking collectives, local(): lax.all_to_all(result.astype(jnp.bfloat16), 'lsec', split_axis=1, concat_...  187 us
    gather x4, local copies, waits for them, and re-layouts, local(): selected_rows = jnp.take(sector_block_list, right_source[term], axis=2)  91.3 us
    dot_general x4, matrix products, weighted_right(): jnp.einsum('vlqbs,qbts->vlqt', selected_rows, scaled, preferred_element_t...  75.3 us
    slice x5, local copies, waits for them, and re-layouts, left_rows(): selected_rows = jnp.take(arranged[:, :, :, term, :], source[term], axis=1)  71.9 us
    dot_general x4, matrix products, left_rows(): jnp.einsum('mbij,vmbjc->vmic', scaled, selected_rows, preferred_element_t...  63.7 us
    reshape x1, local copies, waits for them, and re-layouts, local(): outgoing.reshape(vectors, rows_local, -1)  60.1 us
  transfers between devices with their start and end apart: 3, of which 2 were waited for; matrix products, arithmetic and copies ran while one was open for 12% of the time, Pallas kernels for 0%

commit v1 on v0

--- a/solution.py
+++ b/solution.py
@@ -1,7 +1,17 @@
+import functools
+
 import jax
 import jax.numpy as jnp
 from jax import lax
+from jax.experimental import pallas as pl
+from jax.experimental.pallas import tpu as pltpu
 from jax.sharding import PartitionSpec as P
+
+F32 = jnp.float32
+BF16 = jnp.bfloat16
+I32 = jnp.int32
+WIN = 256
+VMEM_LIMIT = 60 * 1024 * 1024
 
 
 def sector_mask(sizes, tile):
@@ -29,7 +39,7 @@
     return total.reshape(total.shape[0], -1, total.shape[-1])
 
 
-def local(
+def general(
     wavefunction,
     left_tiles,
     left_source_sector,
@@ -98,6 +108,429 @@
     )
 
 
+def exclusive(values):
+    return jnp.cumsum(values, axis=-1) - values
+
+
+def one_hot(index, count):
+    return (index[..., None] == jnp.arange(count, dtype=I32)).astype(BF16)
+
+
+def lookup(table, index):
+    return jnp.sum(jnp.where(index[..., None] == jnp.arange(table.shape[0], dtype=I32), table, 0), axis=-1)
+
+
+def matmul(a, b):
+    return jnp.matmul(a, b, preferred_element_type=F32)
+
+
+def cost(flops, bytes_accessed):
+    return pl.CostEstimate(flops=int(flops), bytes_accessed=int(bytes_accessed), transcendentals=0)
+
+
+def build_kernel(dims, item_kb, item_lo, item_hi, item_win, item_shift, item_size, panel_first, panel_last, right_ref, *outs):
+    widths, right_b, panels = dims
+    tile = right_ref.shape[2]
+    here = pl.program_id(0) * panels + pl.program_id(1)
+    for out in outs:
+        out[...] = jnp.zeros_like(out)
+    lane = lax.broadcasted_iota(I32, (tile, WIN), 1) + pl.program_id(1) * WIN
+    source = lax.broadcasted_iota(I32, (WIN, tile), 1)
+    target = lax.broadcasted_iota(I32, (WIN, tile), 0) - source
+
+    def step(it, carry):
+        kb = item_kb[it]
+        term = kb // right_b
+        block = right_ref[0, kb].astype(F32)
+        block = jnp.where((lane >= item_lo[it]) & (lane < item_hi[it]), block, 0.0).astype(BF16)
+        shift = jnp.where((target == item_shift[it]) & (source < item_size[it]), 1.0, 0.0).astype(BF16)
+        value = jnp.dot(shift, block, preferred_element_type=F32)
+        for part in range(WIN // tile):
+            start = item_win[it] + part * tile
+            base = 0
+            for out, width in zip(outs, widths):
+                @pl.when((start >= base) & (start < base + width))
+                def _(out=out, width=width, base=base):
+                    row = pl.multiple_of(term * width + start - base, tile)
+                    row = jnp.clip(row, 0, out.shape[1] - tile)
+                    row = pl.multiple_of(row, tile)
+                    out[0, pl.ds(row, tile), :] = (
+                        out[0, pl.ds(row, tile), :].astype(F32) + value[part * tile : (part + 1) * tile]
+                    ).astype(BF16)
+                base += width
+        return carry
+
+    lax.fori_loop(panel_first[here], panel_last[here], step, 0)
+
+
+def left_kernel(dims, place_ref, left_slot, left_start, row_start, *refs):
+    chain, terms, steps, width = dims
+    blocks = refs[: 2 * chain - 1]
+    left_ref, out_ref, gathered, left_tiles, sem = refs[2 * chain - 1 :]
+    tile = left_ref.shape[1]
+    place = place_ref[0]
+
+    def each(action):
+        action(pltpu.make_async_copy(blocks[0], gathered.at[place], sem.at[0]))
+        for d in range(1, chain):
+            @pl.when(place - d >= 0)
+            def _():
+                action(pltpu.make_async_copy(blocks[d], gathered.at[jnp.maximum(place - d, 0)], sem.at[d]))
+
+            @pl.when(place + d < chain)
+            def _():
+                action(
+                    pltpu.make_async_copy(
+                        blocks[chain - 1 + d], gathered.at[jnp.minimum(place + d, chain - 1)], sem.at[chain - 1 + d]
+                    )
+                )
+        action(pltpu.make_async_copy(left_ref, left_tiles, sem.at[2 * chain - 1]))
+
+    each(lambda copy: copy.start())
+    out_ref[...] = jnp.zeros_like(out_ref)
+    each(lambda copy: copy.wait())
+
+    def sector_step(sector, carry):
+        row = pl.multiple_of(row_start[sector], 16)
+        for term in range(terms):
+            i = sector * terms + term
+            first_start = pl.multiple_of(left_start[2 * i], 16)
+            second_start = pl.multiple_of(left_start[2 * i + 1], 16)
+            for n in range(0, width, WIN):
+                lanes = slice(n, min(n + WIN, width))
+                value = jnp.dot(
+                    left_tiles[i, :, :WIN],
+                    gathered[left_slot[2 * i], pl.ds(first_start, WIN), lanes],
+                    preferred_element_type=F32,
+                ) + jnp.dot(
+                    left_tiles[i, :, WIN:],
+                    gathered[left_slot[2 * i + 1], pl.ds(second_start, WIN), lanes],
+                    preferred_element_type=F32,
+                )
+                out_ref[pl.ds(row, tile), term * width + n : term * width + lanes.stop] = value.astype(BF16)
+        return carry
+
+    lax.fori_loop(0, steps, sector_step, 0)
+
+
+def right_kernel(dims, half_ref, rows_ref, slot_cols, left_ref, right_ref, *refs):
+    chunk, added = dims
+    out_ref = refs[-1]
+    columns = slot_cols[pl.program_id(0)] - pl.program_id(1) * WIN
+    count = jnp.where(columns > 0, (rows_ref[0] + chunk - 1) // chunk, 0)
+
+    def compute(m, carry):
+        row = pl.multiple_of(m * chunk, chunk)
+        value = jnp.dot(left_ref[pl.ds(row, chunk), :], right_ref[0], preferred_element_type=F32)
+        if added:
+            value = value + refs[0][0, pl.ds(row, chunk), :].astype(F32)
+        out_ref[0, pl.ds(row, chunk), :] = value.astype(BF16)
+        return carry
+
+    def clear(m, carry):
+        row = pl.multiple_of(m * chunk, chunk)
+        out_ref[0, pl.ds(row, chunk), :] = jnp.zeros((chunk, out_ref.shape[2]), BF16)
+        return carry
+
+    lax.fori_loop(0, count, compute, 0)
+    lax.fori_loop(count, out_ref.shape[1] // chunk, clear, 0)
+
+
+def fast(caps, wavefunction, left_tiles, left_source, left_weight, left_sizes, right_tiles, right_source, right_weight, right_sizes):
+    cap_row, cap_pair, cap_half, cap_col = caps
+    vectors, rows_local, cols_local = wavefunction.shape
+    terms, right_local, right_b, tile, _ = right_tiles.shape
+    left_b = left_tiles.shape[2]
+    left_devices = lax.axis_size("lsec")
+    right_devices = lax.axis_size("rsec")
+    left_local = rows_local // tile
+    chain = left_devices // 2
+    height = right_devices // 2
+    left_place = lax.axis_index("lsec")
+    right_place = lax.axis_index("rsec")
+    side = left_place % 2
+    place = left_place // 2
+    core = right_place % 2
+    tall = right_place // 2
+    swap_side = [(i, i ^ 1) for i in range(left_devices)]
+    swap_core = [(i, i ^ 1) for i in range(right_devices)]
+    first_width = (cap_col // 128 + 1) // 2 * 128
+    widths = [first_width, cap_col - first_width]
+    bounds = [0, first_width, cap_col]
+
+    own_sizes = lax.dynamic_slice_in_dim(left_sizes, left_place * left_local, left_local)
+    pair_sizes = left_sizes.reshape(chain, 2 * left_local)
+    pair_offset = exclusive(pair_sizes).reshape(-1)
+    own_count = jnp.sum(own_sizes)
+    rounded = (left_sizes + 15) // 16 * 16
+    half_offset = exclusive(rounded.reshape(left_devices, left_local))
+    half_count = jnp.sum(rounded.reshape(left_devices, left_local), axis=-1)
+    column_offset = exclusive(right_sizes.reshape(right_devices, right_local)).reshape(-1)
+    column_count = jnp.sum(right_sizes.reshape(right_devices, right_local), axis=-1)
+    offsets = jnp.arange(tile, dtype=I32)
+
+    def spread(starts, sizes):
+        return jnp.where(offsets[None, :] < sizes[:, None], starts[:, None] + offsets[None, :], -1).reshape(-1)
+
+    own_right = right_place * right_local
+    col_sizes = lax.dynamic_slice_in_dim(right_sizes, own_right, right_local)
+    col_starts = lax.dynamic_slice_in_dim(column_offset, own_right, right_local)
+    col_select = one_hot(spread(col_starts, col_sizes), cap_col)
+    pair_starts = lax.dynamic_slice_in_dim(pair_offset, left_place * left_local, left_local)
+    local_index = spread(exclusive(own_sizes), own_sizes)
+    pair_index = spread(pair_starts, own_sizes)
+
+    with jax.named_scope("pack"):
+        mine = lax.dynamic_index_in_dim(wavefunction, side, 0, keepdims=False)
+        other = lax.dynamic_index_in_dim(wavefunction, 1 - side, 0, keepdims=False)
+        other_rows = matmul(one_hot(local_index, cap_row).T, other).astype(BF16)
+        mine_rows = matmul(one_hot(pair_index, cap_pair).T, mine).astype(BF16)
+        pair_total = jnp.sum(lax.dynamic_index_in_dim(pair_sizes, place, 0, keepdims=False))
+        partner_base = jnp.where(side == 0, own_count, 0)
+        partner_count = pair_total - own_count
+        spots = jnp.arange(cap_row, dtype=I32)
+        partner_select = one_hot(jnp.where(spots < partner_count, partner_base + spots, -1), cap_pair).T
+        incoming = []
+        for n in range(2):
+            outgoing = matmul(other_rows, col_select[:, bounds[n] : bounds[n + 1]]).astype(BF16)
+            incoming.append(lax.ppermute(outgoing, "lsec", swap_side))
+        pair = []
+        for n in range(2):
+            own_part = matmul(mine_rows, col_select[:, bounds[n] : bounds[n + 1]])
+            pair.append((own_part + matmul(partner_select, incoming[n])).astype(BF16))
+
+    with jax.named_scope("right_exchange"):
+        scaled = (right_tiles.astype(F32) * right_weight[..., None, None]).astype(BF16)
+        compact = jnp.einsum(
+            "kqbts,qtc->kbsc", scaled, col_select.reshape(right_local, tile, cap_col), preferred_element_type=F32
+        ).astype(BF16).reshape(terms * right_b, tile, cap_col)
+        near = jnp.stack([compact, lax.ppermute(compact, "rsec", swap_core)])
+        pieces = []
+        for d in range(1, height):
+            piece = lax.ppermute(
+                compact, "rsec", [(i, ((i // 2 - d) % height) * 2 + i % 2) for i in range(right_devices)]
+            )
+            pieces = pieces + [piece, lax.ppermute(piece, "rsec", swap_core)]
+        far = jnp.stack(pieces) if pieces else None
+
+    with jax.named_scope("left_exchange"):
+        own_weight = lax.dynamic_slice_in_dim(left_weight, left_place * left_local, left_local, 1)
+        left_scaled = (left_tiles.astype(F32) * own_weight[..., None, None]).astype(BF16)
+        left_other = lax.ppermute(left_scaled, "lsec", swap_side)
+        left_pair = jnp.where(
+            side == 0, jnp.concatenate([left_scaled, left_other], 1), jnp.concatenate([left_other, left_scaled], 1)
+        )
+        source = lax.dynamic_slice_in_dim(left_source, place * 2 * left_local, 2 * left_local, 1)
+        source = jnp.transpose(source, (1, 0, 2))
+        source_offset = lookup(pair_offset, source)
+        left_slot = source // (2 * left_local)
+        left_start = jnp.minimum(source_offset // 16 * 16, cap_pair - WIN)
+        source_size = lookup(left_sizes, source)
+        moved = jnp.where(
+            offsets < source_size[..., None], (source_offset - left_start)[..., None] + offsets, -1
+        )
+        left_shifted = jnp.einsum(
+            "klbij,lkbjc->lkibc", left_pair, one_hot(moved, WIN), preferred_element_type=F32
+        ).astype(BF16).reshape(2 * left_local * terms, tile, left_b * WIN)
+
+    with jax.named_scope("chain"):
+        upward = [[part] for part in pair]
+        downward = [[part] for part in pair]
+        for _ in range(1, chain):
+            for n in range(2):
+                upward[n].append(
+                    lax.ppermute(upward[n][-1], "lsec", [(i, i + 2) for i in range(left_devices - 2)])
+                )
+                downward[n].append(
+                    lax.ppermute(downward[n][-1], "lsec", [(i + 2, i) for i in range(left_devices - 2)])
+                )
+
+    with jax.named_scope("lists"):
+        source_all = lax.all_gather(right_source, "rsec", axis=1, tiled=True)
+        source_all = jnp.transpose(source_all.reshape(terms, right_devices, right_local, right_b), (1, 2, 0, 3))
+        slots = jnp.arange(right_devices, dtype=I32)
+        groups = 2 * ((tall + slots // 2) % height) + (core + slots) % 2
+        ordered = jnp.stack(
+            [lax.dynamic_index_in_dim(source_all, groups[s], 0, keepdims=False) for s in range(right_devices)]
+        ).reshape(-1)
+        items = ordered.shape[0]
+        per_sector = terms * right_b
+        per_slot = right_local * per_sector
+        number = jnp.arange(items, dtype=I32)
+        key = jnp.where(ordered // right_local == right_place, number, items + number)
+        key, ordered = lax.sort((key, ordered), num_keys=1)
+        active = key < items
+        number = key % items
+        item_slot = number // per_slot
+        sector = (2 * ((tall + item_slot // 2) % height) + (core + item_slot) % 2) * right_local
+        sector = sector + number // per_sector % right_local
+        low = lookup(column_offset, sector)
+        high = low + lookup(right_sizes, sector)
+        from_offset = lookup(column_offset, ordered)
+        window = jnp.minimum(from_offset // 128 * 128, cap_col - WIN)
+        panels = (cap_col + WIN - 1) // WIN
+        edges = jnp.arange(panels, dtype=I32) * WIN
+        earlier = item_slot[None, None, :] < slots[:, None, None]
+        same = item_slot[None, None, :] == slots[:, None, None]
+        before = active & (earlier | (same & (high <= edges[None, :, None])))
+        within = active & (earlier | (same & (low < edges[None, :, None] + WIN)))
+        panel_first = jnp.sum(before.astype(I32), -1)
+        panel_last = jnp.sum(within.astype(I32), -1)
+        fields = (number % per_sector, low, high, window, from_offset - window, lookup(right_sizes, ordered))
+        halves = lax.dynamic_slice_in_dim(half_offset, place * 2, 2, 0) + jnp.arange(2, dtype=I32)[:, None] * cap_half
+        half_rows = lax.dynamic_slice_in_dim(half_count, place * 2, 2, 0)
+        slot_cols = lookup(column_count, groups)
+
+    anywhere = pl.BlockSpec(memory_space=pl.ANY)
+
+    def build(right_some, from_slot):
+        number_of = right_some.shape[0]
+        scalars = (
+            *fields,
+            panel_first[from_slot : from_slot + number_of].reshape(-1),
+            panel_last[from_slot : from_slot + number_of].reshape(-1),
+        )
+        return pl.pallas_call(
+            functools.partial(build_kernel, (widths, right_b, panels)),
+            out_shape=[jax.ShapeDtypeStruct((number_of, terms * width, cap_col), BF16) for width in widths],
+            grid_spec=pltpu.PrefetchScalarGridSpec(
+                num_scalar_prefetch=len(scalars),
+                grid=(number_of, panels),
+                in_specs=[pl.BlockSpec((1, per_sector, tile, WIN), lambda s, p, *_: (s, 0, 0, p))],
+                out_specs=[pl.BlockSpec((1, terms * width, WIN), lambda s, p, *_: (s, 0, p)) for width in widths],
+            ),
+            compiler_params=pltpu.CompilerParams(vmem_limit_bytes=VMEM_LIMIT),
+            cost_estimate=cost(4e9 * number_of, 20e6 * number_of),
+        )(*scalars, right_some)
+
+    with jax.named_scope("build"):
+        built = [build(near, 0)]
+        if far is not None:
+            built.append(build(far, 2))
+
+    rows = 2 * cap_half
+
+    def apply_left(n):
+        blocks = upward[n] + downward[n][1:]
+        scalars = (place.reshape(1), left_slot.reshape(-1), left_start.reshape(-1), halves.reshape(-1))
+        width = widths[n]
+        return pl.pallas_call(
+            functools.partial(left_kernel, (chain, terms, 2 * left_local, width)),
+            out_shape=jax.ShapeDtypeStruct((rows + tile, terms * width), BF16),
+            grid_spec=pltpu.PrefetchScalarGridSpec(
+                num_scalar_prefetch=len(scalars),
+                grid=(1,),
+                in_specs=[anywhere] * (len(blocks) + 1),
+                out_specs=pl.BlockSpec((rows + tile, terms * width), lambda i, *_: (0, 0)),
+                scratch_shapes=[
+                    pltpu.VMEM((chain, cap_pair, width), BF16),
+                    pltpu.VMEM((2 * left_local * terms, tile, left_b * WIN), BF16),
+                    pltpu.SemaphoreType.DMA((2 * chain,)),
+                ],
+            ),
+            compiler_params=pltpu.CompilerParams(vmem_limit_bytes=VMEM_LIMIT),
+            cost_estimate=cost(15e9, 30e6),
+        )(*scalars, *blocks, left_shifted)
+
+    def apply_right(n, half, product, part, added):
+        number_of = part.shape[0]
+        chunk = 256 if cap_half % 256 == 0 else 128
+        width = terms * widths[n]
+        first_slot = added[1]
+        scalars = (
+            half.reshape(1),
+            lax.dynamic_index_in_dim(half_rows, half, 0),
+            slot_cols[first_slot : first_slot + number_of],
+        )
+        block = pl.BlockSpec((1, cap_half, WIN), lambda s, p, *_: (s, 0, p))
+        extra = [] if added[0] is None else [added[0]]
+        return pl.pallas_call(
+            functools.partial(right_kernel, (chunk, bool(extra))),
+            out_shape=jax.ShapeDtypeStruct((number_of, cap_half, cap_col), BF16),
+            grid_spec=pltpu.PrefetchScalarGridSpec(
+                num_scalar_prefetch=len(scalars),
+                grid=(number_of, panels),
+                in_specs=[
+                    pl.BlockSpec((cap_half, width), lambda s, p, half, *_: (half[0], 0)),
+                    pl.BlockSpec((1, width, WIN), lambda s, p, *_: (s, 0, p)),
+                ]
+                + [block] * len(extra),
+                out_specs=block,
+            ),
+            compiler_params=pltpu.CompilerParams(vmem_limit_bytes=VMEM_LIMIT),
+            cost_estimate=cost(2 * 0.75 * cap_half * width * cap_col * number_of, number_of * width * cap_col * 2),
+        )(*scalars, product, part, *extra)
+
+    def reduce_half(partials):
+        near_sum = partials[0][0].astype(F32) + lax.ppermute(partials[0][1], "rsec", swap_core).astype(F32)
+        result = near_sum
+        if far is not None:
+            from_core = lax.ppermute(partials[1][1::2], "rsec", swap_core)
+            for d in range(1, height):
+                summed = partials[1][2 * d - 2].astype(F32) + from_core[d - 1].astype(F32)
+                result = result + lax.ppermute(
+                    summed.astype(BF16),
+                    "rsec",
+                    [(i, ((i // 2 + d) % height) * 2 + i % 2) for i in range(right_devices)],
+                ).astype(F32)
+        return result.astype(BF16)
+
+    order = [1 - side, side]
+    partials = [[(None, 2 * s) for s in range(len(built))] for _ in order]
+    with jax.named_scope("apply"):
+        for n in range(2):
+            product = apply_left(n)
+            for h in range(2):
+                for s in range(len(built) - 1, -1, -1):
+                    partials[h][s] = (
+                        apply_right(n, order[h], product, built[s][n], partials[h][s]),
+                        2 * s,
+                    )
+    with jax.named_scope("reduce"):
+        given = reduce_half([item[0] for item in partials[0]])
+        taken = lax.ppermute(given, "lsec", swap_side)
+        kept = reduce_half([item[0] for item in partials[1]])
+
+    with jax.named_scope("unpack"):
+        own_half = lax.dynamic_index_in_dim(half_offset, left_place, 0, keepdims=False)
+        row_select = one_hot(spread(own_half, own_sizes), cap_half)
+
+        def expand(value):
+            return matmul(matmul(row_select, value).astype(BF16), col_select.T).astype(BF16)
+
+        kept = expand(kept)
+        taken = expand(taken)
+        return jnp.stack([jnp.where(side == 0, kept, taken), jnp.where(side == 0, taken, kept)])
+
+
+def local(wavefunction, left_tiles, left_source, left_weight, left_sizes, right_tiles, right_source, right_weight, right_sizes):
+    _, rows_local, cols_local = wavefunction.shape
+    left_devices = lax.axis_size("lsec")
+    right_devices = lax.axis_size("rsec")
+    by_device = left_sizes.reshape(left_devices, -1)
+    most_rows = jnp.max(jnp.sum(by_device, -1))
+    most_half = jnp.max(jnp.sum((by_device + 15) // 16 * 16, -1))
+    most_pair = jnp.max(jnp.sum(left_sizes.reshape(left_devices // 2, -1), -1))
+    most_cols = jnp.max(jnp.sum(right_sizes.reshape(right_devices, -1), -1))
+    arguments = (wavefunction, left_tiles, left_source, left_weight, left_sizes, right_tiles, right_source, right_weight, right_sizes)
+    branches = [general]
+    choice = jnp.zeros((), I32)
+    for level, (row, pair, half, col) in enumerate(LEVELS):
+        caps = (
+            rows_local * row // 16,
+            rows_local * pair // 16,
+            rows_local * half // 16,
+            cols_local * col // 16 // 128 * 128,
+        )
+        fits = (most_rows <= caps[0]) & (most_pair <= caps[1]) & (most_half <= caps[2]) & (most_cols <= caps[3])
+        branches.append(functools.partial(fast, caps))
+        choice = jnp.where(fits, level + 1, choice)
+    return lax.switch(choice, branches, *arguments)
+
+
+LEVELS = ((16, 24, 16, 12), (12, 20, 12, 10))
+
+
 def solution(mesh):
     return jax.shard_map(
         local,

time: 2070 us -> 838 us (0.40)
  the two profiles are of different devices: /device:TPU:0 before, /device:TPU:8 now
where the time goes in v1:
time: 838 us; the launch traced here: 823 us
  Pallas kernels  280 us (33%)
  waiting for transfers between devices  169 us (20%)
  matrix products  93.1 us (11%)
  blocking collectives  80 us (10%)
  starting transfers between devices  53.8 us (6%)
  other arithmetic  50.7 us (6%)
  local copies, waits for them, and re-layouts  48.4 us (6%)
  loops' own time  29.2 us (3%)
  between operations  19.1 us (2%)
    pallas_call x8, Pallas kernels, apply_right(): pl.pallas_call(functools.partial(right_kernel, (chunk, bool(extra))), out...  151 us
    pallas_call x2, Pallas kernels, build(): pl.pallas_call(functools.partial(build_kernel, (widths, right_b, panels))...  90.9 us
    all_gather x1, blocking collectives, fast(): source_all = lax.all_gather(right_source, 'rsec', axis=1, tiled=True)  80 us
    ppermute x2, waiting for transfers between devices, reduce_half(): lax.ppermute(summed.astype(BF16), 'rsec', [(i, (i // 2 + d) % height * 2...  75.6 us
    dot_general x12, matrix products, matmul(): return jnp.matmul(a, b, preferred_element_type=F32)  68.4 us
    ppermute x6, waiting for transfers between devices, fast(): lax.ppermute(upward[n][-1], 'lsec', [(i, i + 2) for i in range(left_devic...  66.3 us
    pallas_call x2, Pallas kernels, apply_left(): pl.pallas_call(functools.partial(left_kernel, (chain, terms, 2 * left_loc...  37.7 us
    another operation x1, loops' own time, local(): return lax.switch(choice, branches, *arguments)  29.2 us
  transfers between devices with their start and end apart: 25, of which 8 were waited for; matrix products, arithmetic and copies ran while one was open for 17% of the time, Pallas kernels for 34%

profile of v1, /device:TPU:8, one launch (start us, length us, event | category | flops | bytes accessed | tf_op | source)
XLA Modules:
  0.0 823.1 jit_solution(6235855195595078039)
XLA Ops:
  17.1 798.7 %conditional.1 = (bf16[2,1024,2048]{2,1,0:T(8,128)(2,1)}) conditional(s32[]{:T(128)} %clamp.11, (s32[64]{0:T(128)}, s32[64]{0:T(128)}, bf16[4,16,4,128,128]{4,3,2,1,0:T(8,128)(2,1)}, f32[4,16,4]{1,2,0:T(4,128)}, bf16[2,1024,2048]{2,1,0:T(8,128)(2,1)}, /*index=5*/s32[4,16,4]{1,2,0:T(4,128)}, s32[4,64,2]{1,2,0:T(2,128)}, ...), branch_computations={%region_8.11_spmd, %region_9.30_spmd, %region_28.49_spmd} | conditional | flops 227051995136 | bytes 1910650496 | solution.py:528
  38.5 11.4 %copy.371 = bf16[4,16,4,128,128]{3,4,1,2,0:T(8,128)(2,1)} copy(bf16[4,16,4,128,128]{4,3,2,1,0:T(8,128)(2,1)} %get-tuple-element.273) | data formatting | bytes 16777216 | tf_op jit(solution)/shard_map
  49.9 16.5 %bitcast_convert_fusion.1 = bf16[4,4,128,1280]{3,2,1,0:T(8,128)(2,1)} fusion(bf16[4,16,4,128,128]{3,4,1,2,0:T(8,128)(2,1)} %copy.371, f32[4,16,4]{1,2,0:T(4,128)S(1)} %copy-done.42, s32[16,128]{1,0:T(8,128)S(1)} %get-tuple-element.384), kind=kOutput, calls=%fused_computation.235 | convolution fusion | flops 10755244032 | bytes 13640704 | tf_op jit(solution)/shard_map/cond/branch_2_fun/right_exchange/kqbts,qtc->kbsc/dot_general | solution.py:304
  69.6 2.7 iota_compare_fusion.46
  73.0 6.4 fusion.141
  79.5 3.9 fusion.155
  87.3 5.8 fusion.158
  102.9 80.0 %all_gather.11 = s32[4,64,4]{2,0,1:T(4,128)S(1)} all-gather(s32[4,16,4]{2,0,1:T(4,128)S(1)} %copy.370), channel_id=1, replica_groups=mesh['lsec'=8,'rsec'=4] {'rsec'}, dimensions={1}, use_global_device_ids=true | all-gather | bytes 5120 | tf_op jit(solution)/shard_map/cond/branch_2_fun/lists/all_gather | solution.py:349
  185.9 10.4 %convolution_convert_fusion.1 = bf16[1280,2048]{1,0:T(8,128)(2,1)} fusion(bf16[2,1024,2048]{2,1,0:T(8,128)(2,1)} %get-tuple-element.96, s32[]{:T(128)S(6)} %select_n.555, s32[1024]{0:T(1024)S(1)} %get-tuple-element.389), kind=kOutput, calls=%fused_computation.243 | convolution fusion | flops 5372641280 | bytes 9441284 | tf_op jit(solution)/shard_map/cond/branch_2_fun/pack/dot_general | solution.py:124
  196.6 6.2 fusion.129
  202.9 4.4 fusion.145.refs_0_
  207.3 3.6 collective-permute-start.26
  211.0 8.4 %fusion.125 = f32[1280,640]{1,0:T(8,128)} fusion(bf16[1280,2048]{1,0:T(8,128)(2,1)} %convolution_convert_fusion.1, pred[2048,1280]{1,0:T(32,128)(4,1)S(1)} %copy-done.14), kind=kOutput, calls=%fused_computation.268 | convolution fusion | flops 3355443200 | bytes 9830400 | tf_op jit(solution)/shard_map/cond/branch_2_fun/pack/dot_general | solution.py:124
  220.3 4.4 sort.45
  224.7 3.5 collective-permute-start.29
  228.2 4.2 fusion.144.refs_0_
  232.4 2.3 collective-permute-start.35
  234.8 13.3 %collective-permute-done.26.refs_1_ = bf16[1280,640]{1,0:T(8,128)(2,1)} collective-permute-done((bf16[1280,640]{1,0:T(8,128)(2,1)}, bf16[1280,640]{1,0:T(8,128)(2,1)}, u32[]{:S(2)}, u32[]{:S(2)}) %collective-permute-start.26) | collective-permute-done | bytes 1638432 | tf_op jit(solution)/shard_map/cond/branch_2_fun/chain/ppermute | solution.py:342
  248.1 1.9 collective-permute-start.38
  251.7 13.8 %collective-permute-done.29.refs_4_ = bf16[1280,640]{1,0:T(8,128)(2,1)S(1)} collective-permute-done((bf16[1280,640]{1,0:T(8,128)(2,1)}, bf16[1280,640]{1,0:T(8,128)(2,1)S(1)}, u32[]{:S(2)}, u32[]{:S(2)}) %collective-permute-start.29) | collective-permute-done | bytes 1638432 | tf_op jit(solution)/shard_map/cond/branch_2_fun/chain/ppermute | solution.py:345
  265.5 3.5 collective-permute-start.27
  269.3 13.9 %collective-permute-done.35.refs_1_ = bf16[1280,640]{1,0:T(8,128)(2,1)} collective-permute-done((bf16[1280,640]{1,0:T(8,128)(2,1)S(1)}, bf16[1280,640]{1,0:T(8,128)(2,1)}, u32[]{:S(2)}, u32[]{:S(2)}) %collective-permute-start.35) | collective-permute-done | bytes 1638432 | tf_op jit(solution)/shard_map/cond/branch_2_fun/chain/ppermute | solution.py:342
  283.2 3.5 collective-permute-start.36
  286.7 13.1 %collective-permute-done.38.refs_4_ = bf16[1280,640]{1,0:T(8,128)(2,1)} collective-permute-done((bf16[1280,640]{1,0:T(8,128)(2,1)S(1)}, bf16[1280,640]{1,0:T(8,128)(2,1)}, u32[]{:S(2)}, u32[]{:S(2)}) %collective-permute-start.38) | collective-permute-done | bytes 1638432 | tf_op jit(solution)/shard_map/cond/branch_2_fun/chain/ppermute | solution.py:345
  299.8 3.5 collective-permute-start.39
  304.7 13.4 %collective-permute-done.27.refs_2_ = bf16[1280,640]{1,0:T(8,128)(2,1)S(1)} collective-permute-done((bf16[1280,640]{1,0:T(8,128)(2,1)}, bf16[1280,640]{1,0:T(8,128)(2,1)S(1)}, u32[]{:S(2)}, u32[]{:S(2)}) %collective-permute-start.27) | collective-permute-done | bytes 1638432 | tf_op jit(solution)/shard_map/cond/branch_2_fun/chain/ppermute | solution.py:342
  319.4 1.9 collective-permute-start.30
  327.1 25.7 %collective-permute-done.36.refs_2_ = bf16[1280,640]{1,0:T(8,128)(2,1)} collective-permute-done((bf16[1280,640]{1,0:T(8,128)(2,1)}, bf16[1280,640]{1,0:T(8,128)(2,1)}, u32[]{:S(2)}, u32[]{:S(2)}) %collective-permute-start.36) | collective-permute-done | bytes 1638432 | tf_op jit(solution)/shard_map/cond/branch_2_fun/chain/ppermute | solution.py:342
  352.8 3.5 collective-permute-start.37
  356.3 3.5 collective-permute-start.40
  359.9 8.3 %fusion.104 = bf16[16,4,2,256,128]{4,3,2,1,0:T(8,128)(2,1)} fusion(s32[16,4,2,128]{3,2,1,0:T(2,128)S(1)} %compare_select_fusion.11, bf16[4,8,2,128,128]{4,3,2,0,1:T(8,128)(2,1)} %collective-permute-done.32, bf16[4,8,2,128,128]{4,3,2,0,1:T(8,128)(2,1)} %multiply_convert_fusion.9, pred[]{:T(512)S(6)} %eq.250), kind=kOutput, calls=%fused_computation.244 | convolution fusion | flops 1088421888 | bytes 12648449 | tf_op jit(solution)/shard_map/cond/branch_2_fun/left_exchange/klbij,lkbjc->lkibc/dot_general | solution.py:332
  368.2 12.0 %copy.393.refs_7_ = bf16[64,128,512]{2,1,0:T(8,128)(2,1)} copy(bf16[64,128,512]{1,2,0:T(8,128)(2,1)} %bitcast.468) | data formatting | bytes 16777216 | tf_op jit(solution)/shard_map/cond/branch_2_fun/left_exchange/reshape | solution.py:334
  380.2 2.5 collective-permute-start.28
  382.7 3.6 collective-permute-start.31
  386.5 8.9 %pad_maximum_fusion.3.right_ref = bf16[2,16,128,1280]{3,2,1,0:T(8,128)(2,1)} fusion(bf16[1,16,128,1280]{3,2,1,0:T(8,128)(2,1)} %bitcast.164, bf16[1,16,128,1280]{3,2,1,0:T(8,128)(2,1)} %bitcast.162), kind=kLoop, calls=%fused_computation.233 | loop fusion | flops 5242880 | bytes 20971520 | tf_op jit(solution)/shard_map/cond/branch_2_fun/right_exchange/stack | solution.py:307
  395.3 47.2 %build.6 = (bf16[2,2560,1280]{2,1,0:T(8,128)(2,1)}, bf16[2,2560,1280]{2,1,0:T(8,128)(2,1)}) custom-call(s32[1024]{0:T(1024)} %get-tuple-element.378.item_kb, s32[1024]{0:T(1024)} %copy-done.29, s32[1024]{0:T(1024)} %copy-done.38, s32[1024]{0:T(1024)} %get-tuple-element.381.item_win, s32[1024]{0:T(1024)} %get-tuple-element.380.item_shift, ...), custom_call_target="tpu_custom_call" | custom-call | flops 8000000000 | bytes 40000000 | tf_op jit(solution)/shard_map/cond/branch_2_fun/build/pallas_call | solution.py:393
  442.5 18.8 %apply.31.left_ref = bf16[1664,2560]{1,0:T(8,128)(2,1)} custom-call(s32[1]{0:T(128)} %bitcast.138.place_ref, s32[128]{0:T(128)} %reshape.1147.left_slot, s32[128]{0:T(128)} %multiply_minimum_fusion.1.left_start, s32[16]{0:T(128)} %reshape.1149.row_start, bf16[1280,640]{1,0:T(8,128)(2,1)} %copy-done.49, bf16[1280,640]{1,0:T(8,128)(2,1)} %collective-permute-done.35.refs_1_, ...), custom_call_target="tpu_custom_call" | custom-call | flops 15000000512 | bytes 30000000 | tf_op jit(solution)/shard_map/cond/branch_2_fun/apply/pallas_call | solution.py:417
  461.3 18.8 %apply.36.refs_0_ = bf16[2,768,1280]{2,1,0:T(8,128)(2,1)} custom-call(s32[1]{0:T(128)} %bitcast.171.half_ref, s32[1]{0:T(128)} %get-tuple-element.387.rows_ref, s32[2]{0:T(128)} %get-tuple-element.391.slot_cols, bf16[1664,2560]{1,0:T(8,128)(2,1)} %apply.31.left_ref, bf16[2,2560,1280]{2,1,0:T(8,128)(2,1)} %get-tuple-element.105.right_ref), custom_call_target="tpu_custom_call" | custom-call | flops 7549747200 | bytes 13107200 | tf_op jit(solution)/shard_map/cond/branch_2_fun/apply/pallas_call | solution.py:447
  481.3 18.9 %apply.30.left_ref = bf16[1664,2560]{1,0:T(8,128)(2,1)} custom-call(s32[1]{0:T(128)} %bitcast.138.place_ref, s32[128]{0:T(128)} %reshape.1147.left_slot, s32[128]{0:T(128)} %multiply_minimum_fusion.1.left_start, s32[16]{0:T(128)} %reshape.1149.row_start, bf16[1280,640]{1,0:T(8,128)(2,1)} %fusion.145.refs_0_, ...), custom_call_target="tpu_custom_call" | custom-call | flops 15000000512 | bytes 30000000 | tf_op jit(solution)/shard_map/cond/branch_2_fun/apply/pallas_call | solution.py:417
  500.2 19.1 %apply.37 = bf16[2,768,1280]{2,1,0:T(8,128)(2,1)} custom-call(s32[1]{0:T(128)} %bitcast.171.half_ref, s32[1]{0:T(128)} %get-tuple-element.387.rows_ref, s32[2]{0:T(128)} %get-tuple-element.391.slot_cols, bf16[1664,2560]{1,0:T(8,128)(2,1)} %apply.30.left_ref, bf16[2,2560,1280]{2,1,0:T(8,128)(2,1)} %get-tuple-element.104.right_ref, ...), custom_call_target="tpu_custom_call" | custom-call | flops 7549747200 | bytes 13107200 | tf_op jit(solution)/shard_map/cond/branch_2_fun/apply/pallas_call | solution.py:447
  519.3 3.0 slice_bitcast_fusion.5
  522.3 18.8 %apply.32.refs_0_ = bf16[2,768,1280]{2,1,0:T(8,128)(2,1)} custom-call(s32[1]{0:T(128)} %bitcast.137.half_ref, s32[1]{0:T(128)} %get-tuple-element.386.rows_ref, s32[2]{0:T(128)} %get-tuple-element.391.slot_cols, bf16[1664,2560]{1,0:T(8,128)(2,1)} %apply.31.left_ref, bf16[2,2560,1280]{2,1,0:T(8,128)(2,1)} %get-tuple-element.105.right_ref), custom_call_target="tpu_custom_call" | custom-call | flops 7549747200 | bytes 13107200 | tf_op jit(solution)/shard_map/cond/branch_2_fun/apply/pallas_call | solution.py:447
  541.1 9.0 %pad_maximum_fusion.4.right_ref = bf16[2,16,128,1280]{3,2,1,0:T(8,128)(2,1)} fusion(bf16[1,16,128,1280]{3,2,1,0:T(8,128)(2,1)} %bitcast.169, bf16[1,16,128,1280]{3,2,1,0:T(8,128)(2,1)} %bitcast.168), kind=kLoop, calls=%fused_computation.234 | loop fusion | flops 5242880 | bytes 20971520 | tf_op jit(solution)/shard_map/cond/branch_2_fun/right_exchange/stack | solution.py:314
  550.1 43.7 %build.7 = (bf16[2,2560,1280]{2,1,0:T(8,128)(2,1)}, bf16[2,2560,1280]{2,1,0:T(8,128)(2,1)}) custom-call(s32[1024]{0:T(1024)} %get-tuple-element.378.item_kb, s32[1024]{0:T(1024)} %copy-done.29, s32[1024]{0:T(1024)} %copy-done.38, s32[1024]{0:T(1024)} %get-tuple-element.381.item_win, s32[1024]{0:T(1024)} %get-tuple-element.380.item_shift, ...), custom_call_target="tpu_custom_call" | custom-call | flops 8000000000 | bytes 40000000 | tf_op jit(solution)/shard_map/cond/branch_2_fun/build/pallas_call | solution.py:393
  593.8 18.8 %apply.38.refs_0_ = bf16[2,768,1280]{2,1,0:T(8,128)(2,1)} custom-call(s32[1]{0:T(128)} %bitcast.171.half_ref, s32[1]{0:T(128)} %get-tuple-element.387.rows_ref, s32[2]{0:T(128)} %get-tuple-element.392.slot_cols, bf16[1664,2560]{1,0:T(8,128)(2,1)} %apply.31.left_ref, bf16[2,2560,1280]{2,1,0:T(8,128)(2,1)} %get-tuple-element.107.right_ref), custom_call_target="tpu_custom_call" | custom-call | flops 7549747200 | bytes 13107200 | tf_op jit(solution)/shard_map/cond/branch_2_fun/apply/pallas_call | solution.py:447
  612.6 19.1 %apply.39 = bf16[2,768,1280]{2,1,0:T(8,128)(2,1)} custom-call(s32[1]{0:T(128)} %bitcast.171.half_ref, s32[1]{0:T(128)} %get-tuple-element.387.rows_ref, s32[2]{0:T(128)} %get-tuple-element.392.slot_cols, bf16[1664,2560]{1,0:T(8,128)(2,1)} %apply.30.left_ref, bf16[2,2560,1280]{2,1,0:T(8,128)(2,1)} %get-tuple-element.106.right_ref, ...), custom_call_target="tpu_custom_call" | custom-call | flops 7549747200 | bytes 13107200 | tf_op jit(solution)/shard_map/cond/branch_2_fun/apply/pallas_call | solution.py:447
  631.6 3.0 slice.249
  634.6 3.7 collective-permute-start.47
  638.3 18.7 %apply.34.refs_0_ = bf16[2,768,1280]{2,1,0:T(8,128)(2,1)} custom-call(s32[1]{0:T(128)} %bitcast.137.half_ref, s32[1]{0:T(128)} %get-tuple-element.386.rows_ref, s32[2]{0:T(128)} %get-tuple-element.392.slot_cols, bf16[1664,2560]{1,0:T(8,128)(2,1)} %apply.31.left_ref, bf16[2,2560,1280]{2,1,0:T(8,128)(2,1)} %get-tuple-element.107.right_ref), custom_call_target="tpu_custom_call" | custom-call | flops 7549747200 | bytes 13107200 | tf_op jit(solution)/shard_map/cond/branch_2_fun/apply/pallas_call | solution.py:447
  657.0 19.0 %apply.35 = bf16[2,768,1280]{2,1,0:T(8,128)(2,1)} custom-call(s32[1]{0:T(128)} %bitcast.137.half_ref, s32[1]{0:T(128)} %get-tuple-element.386.rows_ref, s32[2]{0:T(128)} %get-tuple-element.392.slot_cols, bf16[1664,2560]{1,0:T(8,128)(2,1)} %apply.30.left_ref, bf16[2,2560,1280]{2,1,0:T(8,128)(2,1)} %get-tuple-element.106.right_ref, ...), custom_call_target="tpu_custom_call" | custom-call | flops 7549747200 | bytes 13107200 | tf_op jit(solution)/shard_map/cond/branch_2_fun/apply/pallas_call | solution.py:447
  676.0 2.9 slice.245
  679.0 3.0 collective-permute-start.44
  681.9 19.2 %apply.33 = bf16[2,768,1280]{2,1,0:T(8,128)(2,1)} custom-call(s32[1]{0:T(128)} %bitcast.137.half_ref, s32[1]{0:T(128)} %get-tuple-element.386.rows_ref, s32[2]{0:T(128)} %get-tuple-element.391.slot_cols, bf16[1664,2560]{1,0:T(8,128)(2,1)} %apply.30.left_ref, bf16[2,2560,1280]{2,1,0:T(8,128)(2,1)} %get-tuple-element.104.right_ref, ...), custom_call_target="tpu_custom_call" | custom-call | flops 7549747200 | bytes 13107200 | tf_op jit(solution)/shard_map/cond/branch_2_fun/apply/pallas_call | solution.py:447
  701.2 2.2 fusion.148
  705.3 1.9 collective-permute-start.41
  707.1 2.1 fusion.147
  710.9 37.4 %collective-permute-done.48 = bf16[768,1280]{1,0:T(8,128)(2,1)S(1)} collective-permute-done((bf16[768,1280]{1,0:T(8,128)(2,1)S(1)}, bf16[768,1280]{1,0:T(8,128)(2,1)S(1)}, u32[]{:S(2)}, u32[]{:S(2)}) %collective-permute-start.48) | collective-permute-done | bytes 1966112 | tf_op jit(solution)/shard_map/cond/branch_2_fun/reduce/ppermute | solution.py:471
  748.3 2.3 fusion.132
  752.2 38.2 %collective-permute-done.45 = bf16[768,1280]{1,0:T(8,128)(2,1)S(1)} collective-permute-done((bf16[768,1280]{1,0:T(8,128)(2,1)S(1)}, bf16[768,1280]{1,0:T(8,128)(2,1)S(1)}, u32[]{:S(2)}, u32[]{:S(2)}) %collective-permute-start.45) | collective-permute-done | bytes 1966112 | tf_op jit(solution)/shard_map/cond/branch_2_fun/reduce/ppermute | solution.py:471
  790.4 2.6 convolution_convert_fusion.3
  793.0 6.2 fusion.137
  799.2 2.4 convolution_convert_fusion.2.clone.7
  801.6 7.6 select_bitcast_fusion.6
  809.1 6.3 pad_maximum_fusion.5
  (162 shorter events, 37.3 us)
Async XLA Ops:
  38.5 11.4 %copy-start.42 = (f32[4,16,4]{1,2,0:T(4,128)S(1)}, f32[4,16,4]{1,2,0:T(4,128)}, u32[]{:S(2)}) copy-start(f32[4,16,4]{1,2,0:T(4,128)} %get-tuple-element.103) | copy-start | bytes 3076 | tf_op jit(solution)/shard_map/cond
  49.9 19.7 %copy-start.36 = (s32[2048]{0:T(1024)}, s32[2048]{0:T(1024)S(1)}, u32[]{:S(2)}) copy-start(s32[2048]{0:T(1024)S(1)} %get-tuple-element.385) | copy-start | bytes 24580 | tf_op jit(solution)/shard_map/cond
  49.9 18.0 %copy-start.28 = (s32[64]{0:T(128)S(1)}, s32[64]{0:T(128)}, u32[]{:S(2)}) copy-start(s32[64]{0:T(128)} %get-tuple-element.93) | copy-start | bytes 772 | tf_op jit(solution)/shard_map/cond
  66.4 316.3 %collective-permute-start.42 = (bf16[16,128,1280]{2,1,0:T(8,128)(2,1)}, bf16[16,128,1280]{2,1,0:T(8,128)(2,1)}, u32[]{:S(2)}, u32[]{:S(2)}) collective-permute-start(bf16[16,128,1280]{2,1,0:T(8,128)(2,1)} %bitcast.163), channel_id=1, source_target_pairs={{0,2},{1,3},{2,0},{3,1},{4,6},{5,7},{6,4},{7,5},{8,10},{9,11},{10,... | collective-permute-start | bytes 15728648 | tf_op jit(solution)/shard_map/cond/branch_2_fun/right_exchange/ppermute | solution.py:310
  67.9 318.5 %collective-permute-start.33 = (bf16[16,128,1280]{2,1,0:T(8,128)(2,1)}, bf16[16,128,1280]{2,1,0:T(8,128)(2,1)}, u32[]{:S(2)}, u32[]{:S(2)}) collective-permute-start(bf16[16,128,1280]{2,1,0:T(8,128)(2,1)} %bitcast.163), channel_id=1, source_target_pairs={{0,1},{1,0},{2,3},{3,2},{4,5},{5,4},{6,7},{7,6},{8,9},{9,8},{10,11... | collective-permute-start | bytes 15728648 | tf_op jit(solution)/shard_map/cond/branch_2_fun/right_exchange/ppermute | solution.py:307
  73.0 6.5 copy-start.13
  79.4 3.9 copy-start.53
  79.5 5.4 copy-start.33
  79.5 5.5 copy-start.5
  83.4 119.5 %collective-permute-start.25 = (bf16[768,640]{1,0:T(8,128)(2,1)}, bf16[768,640]{1,0:T(8,128)(2,1)}, u32[]{:S(2)}, u32[]{:S(2)}) collective-permute-start(bf16[768,640]{1,0:T(8,128)(2,1)} %fusion.155), channel_id=1, source_target_pairs={{0,4},{4,0},{8,12},{12,8},{16,20},{20,16},{24,28},{28,24},{1,5},{5... | collective-permute-start | bytes 2949128 | tf_op jit(solution)/shard_map/cond/branch_2_fun/pack/ppermute | solution.py:296
  86.8 16.0 %copy-start.19 = (s32[4,16,4]{1,2,0:T(4,128)S(1)}, s32[4,16,4]{1,2,0:T(4,128)}, u32[]{:S(2)}) copy-start(s32[4,16,4]{1,2,0:T(4,128)} %get-tuple-element.272) | copy-start | bytes 3076 | tf_op jit(solution)/shard_map/cond
  86.8 145.6 %collective-permute-start.32 = (bf16[4,8,2,128,128]{4,3,2,0,1:T(8,128)(2,1)}, bf16[4,8,2,128,128]{4,3,2,0,1:T(8,128)(2,1)}, u32[]{:S(2)}, u32[]{:S(2)}) collective-permute-start(bf16[4,8,2,128,128]{4,3,2,0,1:T(8,128)(2,1)} %multiply_convert_fusion.9), channel_id=1, source_target_pairs={{0,4},{4,0},{8,12},{12,8},{16,20},{20,16},{24,28},{28,24},{1,5},{5... | collective-permute-start | bytes 6291464 | tf_op jit(solution)/shard_map/cond/branch_2_fun/left_exchange/ppermute | solution.py:319
  93.2 131.6 %collective-permute-start.34 = (bf16[768,640]{1,0:T(8,128)(2,1)}, bf16[768,640]{1,0:T(8,128)(2,1)}, u32[]{:S(2)}, u32[]{:S(2)}) collective-permute-start(bf16[768,640]{1,0:T(8,128)(2,1)} %fusion.158), channel_id=1, source_target_pairs={{0,4},{4,0},{8,12},{12,8},{16,20},{20,16},{24,28},{28,24},{1,5},{5... | collective-permute-start | bytes 2949128 | tf_op jit(solution)/shard_map/cond/branch_2_fun/pack/ppermute | solution.py:296
  185.9 10.8 %copy-start.14 = (pred[2048,1280]{1,0:T(32,128)(4,1)S(1)}, pred[2048,1280]{1,0:T(32,128)(4,1)}, u32[]{:S(2)}) copy-start(pred[2048,1280]{1,0:T(32,128)(4,1)} %iota_compare_fusion.46) | copy-start | bytes 7864324 | tf_op jit(solution)/shard_map/cond
  202.9 8.1 copy-start.22
  207.3 40.8 %collective-permute-start.26 = (bf16[1280,640]{1,0:T(8,128)(2,1)}, bf16[1280,640]{1,0:T(8,128)(2,1)}, u32[]{:S(2)}, u32[]{:S(2)}) collective-permute-start(bf16[1280,640]{1,0:T(8,128)(2,1)} %fusion.145.refs_0_), channel_id=1, source_target_pairs={{0,8},{4,12},{8,16},{12,20},{16,24},{20,28},{1,9},{5,13},{9,17},{1... | collective-permute-start | bytes 4915208 | tf_op jit(solution)/shard_map/cond/branch_2_fun/chain/ppermute | solution.py:342
  219.9 30.7 %copy-start.3 = (s32[64]{0:T(128)S(1)}, s32[64]{0:T(128)}, u32[]{:S(2)}) copy-start(s32[64]{0:T(128)} %get-tuple-element.94) | copy-start | bytes 772 | tf_op jit(solution)/shard_map/cond
  224.7 40.7 %collective-permute-start.29 = (bf16[1280,640]{1,0:T(8,128)(2,1)}, bf16[1280,640]{1,0:T(8,128)(2,1)S(1)}, u32[]{:S(2)}, u32[]{:S(2)}) collective-permute-start(bf16[1280,640]{1,0:T(8,128)(2,1)} %fusion.145.refs_0_), channel_id=1, source_target_pairs={{8,0},{12,4},{16,8},{20,12},{24,16},{28,20},{9,1},{13,5},{17,9},{2... | collective-permute-start | bytes 4915208 | tf_op jit(solution)/shard_map/cond/branch_2_fun/chain/ppermute | solution.py:345
  232.4 72.3 %copy-start.49 = (bf16[1280,640]{1,0:T(8,128)(2,1)}, bf16[1280,640]{1,0:T(8,128)(2,1)S(1)}, u32[]{:S(2)}) copy-start(bf16[1280,640]{1,0:T(8,128)(2,1)S(1)} %fusion.144.refs_0_) | copy-start | bytes 4915204 | tf_op jit(solution)/shard_map/cond
  232.4 50.8 %collective-permute-start.35 = (bf16[1280,640]{1,0:T(8,128)(2,1)S(1)}, bf16[1280,640]{1,0:T(8,128)(2,1)}, u32[]{:S(2)}, u32[]{:S(2)}) collective-permute-start(bf16[1280,640]{1,0:T(8,128)(2,1)S(1)} %fusion.144.refs_0_), channel_id=1, source_target_pairs={{0,8},{4,12},{8,16},{12,20},{16,24},{20,28},{1,9},{5,13},{9,17},{1... | collective-permute-start | bytes 4915208 | tf_op jit(solution)/shard_map/cond/branch_2_fun/chain/ppermute | solution.py:342
  248.1 51.7 %collective-permute-start.38 = (bf16[1280,640]{1,0:T(8,128)(2,1)S(1)}, bf16[1280,640]{1,0:T(8,128)(2,1)}, u32[]{:S(2)}, u32[]{:S(2)}) collective-permute-start(bf16[1280,640]{1,0:T(8,128)(2,1)S(1)} %fusion.144.refs_0_), channel_id=1, source_target_pairs={{8,0},{12,4},{16,8},{20,12},{24,16},{28,20},{9,1},{13,5},{17,9},{2... | collective-permute-start | bytes 4915208 | tf_op jit(solution)/shard_map/cond/branch_2_fun/chain/ppermute | solution.py:345
  251.4 116.8 %copy-start.29 = (s32[1024]{0:T(1024)}, s32[1024]{0:T(1024)S(1)}, u32[]{:S(2)}) copy-start(s32[1024]{0:T(1024)S(1)} %get-tuple-element.290.item_lo) | copy-start | bytes 12292 | tf_op jit(solution)/shard_map/cond
  251.4 116.7 %copy-start.38 = (s32[1024]{0:T(1024)}, s32[1024]{0:T(1024)S(1)}, u32[]{:S(2)}) copy-start(s32[1024]{0:T(1024)S(1)} %add.716.item_hi) | copy-start | bytes 12292 | tf_op jit(solution)/shard_map/cond
  265.5 102.7 %copy-start.48 = (bf16[1280,640]{1,0:T(8,128)(2,1)}, bf16[1280,640]{1,0:T(8,128)(2,1)S(1)}, u32[]{:S(2)}) copy-start(bf16[1280,640]{1,0:T(8,128)(2,1)S(1)} %collective-permute-done.29.refs_4_) | copy-start | bytes 4915204 | tf_op jit(solution)/shard_map/cond
  265.5 52.7 %collective-permute-start.27 = (bf16[1280,640]{1,0:T(8,128)(2,1)}, bf16[1280,640]{1,0:T(8,128)(2,1)S(1)}, u32[]{:S(2)}, u32[]{:S(2)}) collective-permute-start(bf16[1280,640]{1,0:T(8,128)(2,1)} %collective-permute-done.26.refs_1_), channel_id=1, source_target_pairs={{0,8},{4,12},{8,16},{12,20},{16,24},{20,28},{1,9},{5,13},{9,17},{1... | collective-permute-start | bytes 4915208 | tf_op jit(solution)/shard_map/cond/branch_2_fun/chain/ppermute | solution.py:342
  283.2 69.7 %collective-permute-start.36 = (bf16[1280,640]{1,0:T(8,128)(2,1)}, bf16[1280,640]{1,0:T(8,128)(2,1)}, u32[]{:S(2)}, u32[]{:S(2)}) collective-permute-start(bf16[1280,640]{1,0:T(8,128)(2,1)} %collective-permute-done.35.refs_1_), channel_id=1, source_target_pairs={{0,8},{4,12},{8,16},{12,20},{16,24},{20,28},{1,9},{5,13},{9,17},{1... | collective-permute-start | bytes 4915208 | tf_op jit(solution)/shard_map/cond/branch_2_fun/chain/ppermute | solution.py:342
  299.8 56.5 %collective-permute-start.39 = (bf16[1280,640]{1,0:T(8,128)(2,1)}, bf16[1280,640]{1,0:T(8,128)(2,1)}, u32[]{:S(2)}, u32[]{:S(2)}) collective-permute-start(bf16[1280,640]{1,0:T(8,128)(2,1)} %collective-permute-done.38.refs_4_), channel_id=1, source_target_pairs={{8,0},{12,4},{16,8},{20,12},{24,16},{28,20},{9,1},{13,5},{17,9},{2... | collective-permute-start | bytes 4915208 | tf_op jit(solution)/shard_map/cond/branch_2_fun/chain/ppermute | solution.py:345
  318.2 1.2 copy-start.50
  319.4 60.8 %collective-permute-start.30 = (bf16[1280,640]{1,0:T(8,128)(2,1)S(1)}, bf16[1280,640]{1,0:T(8,128)(2,1)}, u32[]{:S(2)}, u32[]{:S(2)}) collective-permute-start(bf16[1280,640]{1,0:T(8,128)(2,1)S(1)} %collective-permute-done.29.refs_4_), channel_id=1, source_target_pairs={{8,0},{12,4},{16,8},{20,12},{24,16},{28,20},{9,1},{13,5},{17,9},{2... | collective-permute-start | bytes 4915208 | tf_op jit(solution)/shard_map/cond/branch_2_fun/chain/ppermute | solution.py:345
  352.8 89.7 %collective-permute-start.37 = (bf16[1280,640]{1,0:T(8,128)(2,1)}, bf16[1280,640]{1,0:T(8,128)(2,1)}, u32[]{:S(2)}, u32[]{:S(2)}) collective-permute-start(bf16[1280,640]{1,0:T(8,128)(2,1)} %collective-permute-done.36.refs_2_), channel_id=1, source_target_pairs={{0,8},{4,12},{8,16},{12,20},{16,24},{20,28},{1,9},{5,13},{9,17},{1... | collective-permute-start | bytes 4915208 | tf_op jit(solution)/shard_map/cond/branch_2_fun/chain/ppermute | solution.py:342
  356.3 86.2 %collective-permute-start.40 = (bf16[1280,640]{1,0:T(8,128)(2,1)}, bf16[1280,640]{1,0:T(8,128)(2,1)}, u32[]{:S(2)}, u32[]{:S(2)}) collective-permute-start(bf16[1280,640]{1,0:T(8,128)(2,1)} %collective-permute-done.39.refs_5_), channel_id=1, source_target_pairs={{8,0},{12,4},{16,8},{20,12},{24,16},{28,20},{9,1},{13,5},{17,9},{2... | collective-permute-start | bytes 4915208 | tf_op jit(solution)/shard_map/cond/branch_2_fun/chain/ppermute | solution.py:345
  368.2 12.0 %copy-start.51 = (bf16[1280,640]{1,0:T(8,128)(2,1)S(1)}, bf16[1280,640]{1,0:T(8,128)(2,1)}, u32[]{:S(2)}) copy-start(bf16[1280,640]{1,0:T(8,128)(2,1)} %copy-done.50) | copy-start | bytes 4915204 | tf_op jit(solution)/shard_map/cond
  380.2 99.9 %collective-permute-start.28 = (bf16[1280,640]{1,0:T(8,128)(2,1)S(1)}, bf16[1280,640]{1,0:T(8,128)(2,1)S(1)}, u32[]{:S(2)}, u32[]{:S(2)}) collective-permute-start(bf16[1280,640]{1,0:T(8,128)(2,1)S(1)} %copy-done.51), channel_id=1, source_target_pairs={{0,8},{4,12},{8,16},{12,20},{16,24},{20,28},{1,9},{5,13},{9,17},{1... | collective-permute-start | bytes 4915208 | tf_op jit(solution)/shard_map/cond/branch_2_fun/chain/ppermute | solution.py:342
  382.7 97.4 %collective-permute-start.31 = (bf16[1280,640]{1,0:T(8,128)(2,1)}, bf16[1280,640]{1,0:T(8,128)(2,1)}, u32[]{:S(2)}, u32[]{:S(2)}) collective-permute-start(bf16[1280,640]{1,0:T(8,128)(2,1)} %collective-permute-done.30.refs_5_), channel_id=1, source_target_pairs={{8,0},{12,4},{16,8},{20,12},{24,16},{28,20},{9,1},{13,5},{17,9},{2... | collective-permute-start | bytes 4915208 | tf_op jit(solution)/shard_map/cond/branch_2_fun/chain/ppermute | solution.py:345
  386.4 154.7 %collective-permute-start.43 = (bf16[16,128,1280]{2,1,0:T(8,128)(2,1)}, bf16[16,128,1280]{2,1,0:T(8,128)(2,1)}, u32[]{:S(2)}, u32[]{:S(2)}) collective-permute-start(bf16[16,128,1280]{2,1,0:T(8,128)(2,1)} %collective-permute-done.42), channel_id=1, source_target_pairs={{0,1},{1,0},{2,3},{3,2},{4,5},{5,4},{6,7},{7,6},{8,9},{9,8},{10,11... | collective-permute-start | bytes 15728648 | tf_op jit(solution)/shard_map/cond/branch_2_fun/right_exchange/ppermute | solution.py:313
  480.1 1.2 copy-start.52
  522.3 188.7 %collective-permute-start.46 = (bf16[768,1280]{1,0:T(8,128)(2,1)}, bf16[768,1280]{1,0:T(8,128)(2,1)}, u32[]{:S(2)}, u32[]{:S(2)}) collective-permute-start(bf16[768,1280]{1,0:T(8,128)(2,1)} %slice_bitcast_fusion.5), channel_id=1, source_target_pairs={{0,1},{1,0},{2,3},{3,2},{4,5},{5,4},{6,7},{7,6},{8,9},{9,8},{10,11... | collective-permute-start | bytes 5898248 | tf_op jit(solution)/shard_map/cond/branch_2_fun/reduce/ppermute | solution.py:465
  634.6 66.6 %collective-permute-start.47 = (bf16[1,768,1280]{2,1,0:T(8,128)(2,1)}, bf16[1,768,1280]{2,1,0:T(8,128)(2,1)}, u32[]{:S(2)}, u32[]{:S(2)}) collective-permute-start(bf16[1,768,1280]{2,1,0:T(8,128)(2,1)} %slice.249), channel_id=1, source_target_pairs={{0,1},{1,0},{2,3},{3,2},{4,5},{5,4},{6,7},{7,6},{8,9},{9,8},{10,11... | collective-permute-start | bytes 5898248 | tf_op jit(solution)/shard_map/cond/branch_2_fun/reduce/ppermute | solution.py:468
  679.0 22.2 %copy-start.7 = (bf16[2,768,1280]{2,1,0:T(8,128)(2,1)S(1)}, bf16[2,768,1280]{2,1,0:T(8,128)(2,1)}, u32[]{:S(2)}) copy-start(bf16[2,768,1280]{2,1,0:T(8,128)(2,1)} %apply.39) | copy-start | bytes 11796484 | tf_op jit(solution)/shard_map/cond
  679.0 28.2 %collective-permute-start.44 = (bf16[1,768,1280]{2,1,0:T(8,128)(2,1)}, bf16[1,768,1280]{2,1,0:T(8,128)(2,1)}, u32[]{:S(2)}, u32[]{:S(2)}) collective-permute-start(bf16[1,768,1280]{2,1,0:T(8,128)(2,1)} %slice.245), channel_id=1, source_target_pairs={{0,1},{1,0},{2,3},{3,2},{4,5},{5,4},{6,7},{7,6},{8,9},{9,8},{10,11... | collective-permute-start | bytes 5898248 | tf_op jit(solution)/shard_map/cond/branch_2_fun/reduce/ppermute | solution.py:468
  701.1 6.0 copy-start.6
  703.3 45.0 %copy-start.8 = (bf16[2,768,1280]{2,1,0:T(8,128)(2,1)S(1)}, bf16[2,768,1280]{2,1,0:T(8,128)(2,1)}, u32[]{:S(2)}) copy-start(bf16[2,768,1280]{2,1,0:T(8,128)(2,1)} %apply.37) | copy-start | bytes 11796484 | tf_op jit(solution)/shard_map/cond
  703.3 44.9 %collective-permute-start.48 = (bf16[768,1280]{1,0:T(8,128)(2,1)S(1)}, bf16[768,1280]{1,0:T(8,128)(2,1)S(1)}, u32[]{:S(2)}, u32[]{:S(2)}) collective-permute-start(bf16[768,1280]{1,0:T(8,128)(2,1)S(1)} %fusion.148), channel_id=1, source_target_pairs={{0,2},{1,3},{2,0},{3,1},{4,6},{5,7},{6,4},{7,5},{8,10},{9,11},{10,... | collective-permute-start | bytes 5898248 | tf_op jit(solution)/shard_map/cond/branch_2_fun/reduce/ppermute | solution.py:471
  705.3 46.9 %collective-permute-start.41 = (bf16[768,1280]{1,0:T(8,128)(2,1)S(1)}, bf16[768,1280]{1,0:T(8,128)(2,1)S(1)}, u32[]{:S(2)}, u32[]{:S(2)}) collective-permute-start(bf16[768,1280]{1,0:T(8,128)(2,1)S(1)} %slice_bitcast_fusion.7), channel_id=1, source_target_pairs={{0,1},{1,0},{2,3},{3,2},{4,5},{5,4},{6,7},{7,6},{8,9},{9,8},{10,11... | collective-permute-start | bytes 5898248 | tf_op jit(solution)/shard_map/cond/branch_2_fun/reduce/ppermute | solution.py:465
  709.2 81.2 %copy-start.9 = (bf16[2,768,1280]{2,1,0:T(8,128)(2,1)S(1)}, bf16[2,768,1280]{2,1,0:T(8,128)(2,1)}, u32[]{:S(2)}) copy-start(bf16[2,768,1280]{2,1,0:T(8,128)(2,1)} %apply.33) | copy-start | bytes 11796484 | tf_op jit(solution)/shard_map/cond
  709.3 81.2 %copy-start.44 = (s32[1024]{0:T(1024)S(1)}, s32[1024]{0:T(1024)}, u32[]{:S(2)}) copy-start(s32[1024]{0:T(1024)} %get-tuple-element.388) | copy-start | bytes 12292 | tf_op jit(solution)/shard_map/cond
  709.3 81.2 %collective-permute-start.45 = (bf16[768,1280]{1,0:T(8,128)(2,1)S(1)}, bf16[768,1280]{1,0:T(8,128)(2,1)S(1)}, u32[]{:S(2)}, u32[]{:S(2)}) collective-permute-start(bf16[768,1280]{1,0:T(8,128)(2,1)S(1)} %fusion.147), channel_id=1, source_target_pairs={{0,2},{1,3},{2,0},{3,1},{4,6},{5,7},{6,4},{7,5},{8,10},{9,11},{10,... | collective-permute-start | bytes 5898248 | tf_op jit(solution)/shard_map/cond/branch_2_fun/reduce/ppermute | solution.py:471
  750.6 48.6 %collective-permute-start.49 = (bf16[768,1280]{1,0:T(8,128)(2,1)S(1)}, bf16[768,1280]{1,0:T(8,128)(2,1)S(1)}, u32[]{:S(2)}, u32[]{:S(2)}) collective-permute-start(bf16[768,1280]{1,0:T(8,128)(2,1)S(1)} %fusion.132), channel_id=1, source_target_pairs={{0,4},{4,0},{8,12},{12,8},{16,20},{20,16},{24,28},{28,24},{1,5},{5... | collective-permute-start | bytes 5898248 | tf_op jit(solution)/shard_map/cond/branch_2_fun/reduce/ppermute | solution.py:491
  790.4 2.6 copy-start.37
